TPU v7x, 1024 devices: a whole 8x8x8 slice. The times are simulated.
1024 devices in a mesh: fsdp: 64 (over z, x), tp: 16 (over y, core).
Axes of the slice: x: 8, y: 8, z: 8, core: 2. Of those that a mesh axis runs over, the one named last changes fastest.
Arguments:
- momentum: float32 [7168, 18432], P('fsdp', 'tp'), may hold values from -6 to 6
- gradient: bfloat16 [7168, 18432], P('fsdp', 'tp'), may hold values from -6 to 6
- factor: float32 [18432, 448], P('tp'), may hold values from -0.046875 to 0.046875
Outputs:
- new_momentum: float32 [7168, 18432], P('fsdp', 'tp')
- update: float32 [7168, 18432], P('fsdp', 'tp')
- new_factor: float32 [18432, 448], P('tp')
All inputs are finite; a program needn't handle non-finite values.
Results may differ from a plain program's by a relative error of at most 0.0003.
Values sent between devices are 32-bit elements; how exact they have to be, the bound alone decides.
A program may use at most 64 MiB of HBM per device.

v0:
```python
import math

import jax
import jax.numpy as jnp
from jax import lax
from jax.sharding import PartitionSpec as P

M_ROWS = 7168
N_COLS = 18432
RANK = 448


momentum_decay = 0.95
epsilon = 1e-08


def mult(left, right):
    return jnp.dot(left, right, precision=lax.Precision.HIGHEST)


def make_orthonormal(triangle, rows_block):
    return jax.scipy.linalg.solve_triangular(triangle, rows_block.T, lower=True).T


def per_device(momentum, gradient, factor):
    buffer = momentum + gradient.astype(jnp.float32)
    partial_rows = mult(buffer, factor)
    projected = lax.psum(partial_rows, "tp")
    inner = lax.psum(mult(projected.T, projected), "fsdp")
    triangle = jnp.linalg.cholesky(inner)
    orthonormal = make_orthonormal(triangle, projected)
    right_rows = lax.psum_scatter(
        mult(buffer.T, orthonormal), "fsdp", scatter_dimension=0, tiled=True
    )
    column_norms = jnp.sqrt(
        lax.psum(jnp.sum(right_rows * right_rows, axis=0), ("fsdp", "tp")) + epsilon
    )
    factor_rows = right_rows / column_norms
    gathered = lax.all_gather(factor_rows, "fsdp", axis=0, tiled=True)
    new_momentum = buffer - (1.0 - momentum_decay) * mult(orthonormal, (gathered * column_norms).T)
    scale_factor = math.sqrt(M_ROWS * N_COLS / RANK)
    update = scale_factor * mult(orthonormal, gathered.T)
    return (new_momentum, update, gathered)


def solution(mesh):
    in_specs = (P("fsdp", "tp"), P("fsdp", "tp"), P("tp", None))
    out_specs = (P("fsdp", "tp"), P("fsdp", "tp"), P("tp", None))
    return jax.shard_map(
        per_device, mesh=mesh, in_specs=in_specs, out_specs=out_specs, check_vma=False
    )
```

profile of v0, /device:TPU:1, one launch (start us, length us, event | category | flops | bytes accessed | tf_op | source)
XLA Modules:
  0.0 860.6 jit_solution(11757840219823852992)
XLA Ops:
  7.2 1.5 copy-done
  8.8 3.8 fusion.5
  12.6 131.6 %all-reduce.8.cloned.1.call-done = f32[112,448]{1,0:T(8,128)} async-done(((f32[112,448]{1,0:T(8,128)}), f32[112,448]{1,0:T(8,128)}) %all-reduce.8.cloned.1.call-update) | async-done | bytes 200720 | tf_op jit(solution)/shard_map/psum | solution.py:28
  144.2 2.9 fusion.40
  148.0 168.5 %all-reduce.10.cloned.1.call-done = f32[448,448]{0,1:T(8,128)} async-done(((f32[448,448]{0,1:T(8,128)}), f32[448,448]{0,1:T(8,128)}) %all-reduce.10.cloned.1.call-update) | async-done | bytes 802832 | tf_op jit(solution)/shard_map/psum | solution.py:29
  316.5 2.5 copy.15
  319.0 1.4 fusion.3
  321.3 11.7 %cholesky.105 = f32[128,128]{1,0:T(8,128)S(1)} custom-call(f32[128,128]{1,0:T(8,128)S(1)} %cholesky.272), custom_call_target="Cholesky" | custom-call | tf_op jit(solution)/shard_map/jit(cholesky)/cholesky | solution.py:30
  333.0 9.8 %custom-call.31 = f32[1,128,128]{1,2,0:T(8,128)S(1)} custom-call(f32[1,128,128]{2,1,0:T(8,128)S(1)} %get-tuple-element.37), custom_call_target="InvertDiagBlocksLowerTriangular" | custom-call | tf_op jit(solution)/shard_map/jit(cholesky)/cholesky | solution.py:30
  343.0 1.2 constant_dynamic-update-slice_fusion.3
  344.2 1.2 convolution_subtract_fusion
  345.4 11.7 %cholesky.219 = f32[128,128]{1,0:T(8,128)S(1)} custom-call(f32[128,128]{1,0:T(8,128)S(1)} %cholesky.276), custom_call_target="Cholesky" | custom-call | tf_op jit(solution)/shard_map/jit(cholesky)/cholesky | solution.py:30
  357.2 10.0 %custom-call.32 = f32[1,128,128]{1,2,0:T(8,128)S(1)} custom-call(f32[1,128,128]{2,1,0:T(8,128)S(1)} %get-tuple-element.34), custom_call_target="InvertDiagBlocksLowerTriangular" | custom-call | tf_op jit(solution)/shard_map/jit(cholesky)/cholesky | solution.py:30
  367.4 1.2 convolution_subtract_fusion.1
  368.7 11.7 %cholesky.240 = f32[128,128]{1,0:T(8,128)S(1)} custom-call(f32[128,128]{1,0:T(8,128)S(1)} %cholesky.281), custom_call_target="Cholesky" | custom-call | tf_op jit(solution)/shard_map/jit(cholesky)/cholesky | solution.py:30
  381.1 9.8 %custom-call.33 = f32[1,128,128]{1,2,0:T(8,128)S(1)} custom-call(f32[1,128,128]{2,1,0:T(8,128)S(1)} %get-tuple-element.31), custom_call_target="InvertDiagBlocksLowerTriangular" | custom-call | tf_op jit(solution)/shard_map/jit(cholesky)/cholesky | solution.py:30
  392.1 5.8 cholesky.260
  402.9 10.7 %while.1 = (s32[]{:T(128)}, f32[448,448]{1,0:T(8,128)}, s32[3,2]{0,1:T(2,128)S(1)}, f32[3,128,128]{2,1,0:T(8,128)}, s32[]{:T(128)}) while((s32[]{:T(128)}, f32[448,448]{1,0:T(8,128)}, s32[3,2]{0,1:T(2,128)S(1)}, f32[3,128,128]{2,1,0:T(8,128)}, s32[]{:T(128)}) %tuple.45), condition=%wide.while_cond, body=%wide.while_body.sunk | while | flops 2 | bytes 132205 | solution.py:22
  403.6 2.9 bitcast_dynamic-update-slice_fusion.2
  407.1 2.9 bitcast_dynamic-update-slice_fusion.2
  410.7 2.9 bitcast_dynamic-update-slice_fusion.2
  415.5 39.3 %custom-call.34 = f32[4,128,128]{1,2,0:T(8,128)S(1)} custom-call(f32[4,128,128]{2,1,0:T(8,128)S(1)} %pad_maximum_fusion), custom_call_target="InvertDiagBlocksLowerTriangular" | custom-call | tf_op jit(solution)/shard_map/jit(_solve_triangular)/triangular_solve | solution.py:22
  459.9 3.5 fusion.4
  463.5 1.3 dynamic-slice.3
  465.4 172.9 %all-reduce.12.cloned.1.call-done = f32[1152,448]{1,0:T(8,128)} async-done(((f32[1152,448]{1,0:T(8,128)}), f32[1152,448]{1,0:T(8,128)}) %all-reduce.12.cloned.1.call-update) | async-done | bytes 2064400
  639.2 115.1 %psum.23 = f32[448]{0:T(512)S(1)} all-reduce(f32[448]{0:T(512)S(1)} %multiply_reduce_fusion), channel_id=1, replica_groups=mesh['fsdp'=64,'tp'=16] {'fsdp','tp'}, use_global_device_ids=true, to_apply=%region_12.13 | all-reduce | flops 448 | bytes 3584 | tf_op jit(solution)/shard_map/psum | solution.py:36
  754.3 1.5 divide_bitcast_fusion
  755.8 83.6 %all-gather.3.cloned.1.call-done = f32[64,18,448]{2,1,0:T(8,128)} async-done(((f32[1,18,448]{2,1,0:T(8,128)}), f32[64,18,448]{2,1,0:T(8,128)}) %all-gather.3.cloned.1.call-update) | async-done | bytes 2064400 | tf_op jit(solution)/shard_map/all_gather | solution.py:39
  839.4 3.6 reshape.69
  843.0 4.9 fusion
  847.9 3.2 convolution_multiply_fusion
  851.1 2.9 copy.18
  (59 shorter events, 16.6 us)
Async XLA Ops:
  7.2 1.6 copy-start
  7.2 137.0 %all-reduce.8.cloned.1.call-start = ((), (), s32[]{:S(2)}) async-start(), calls=%async_computation | async-start | bytes 458752 | tf_op jit(solution)/shard_map/psum | solution.py:28
  12.6 303.9 %all-reduce.10.cloned.1.call-start = ((), (), s32[]{:S(2)}) async-start(), calls=%async_computation.1 | async-start | bytes 1835008 | tf_op jit(solution)/shard_map/psum | solution.py:29
  147.1 491.2 %all-reduce.12.cloned.1.call-start = ((), (), s32[]{:S(2)}) async-start(), calls=%async_computation.3 | async-start | bytes 4718592
  316.5 2.5 copy-start.3
  320.3 0.9 copy-start.6
  401.9 58.1 %copy-start.2 = (f32[112,1152]{1,0:T(8,128)S(1)}, f32[112,1152]{1,0:T(8,128)}, u32[]{:S(2)}) copy-start(f32[112,1152]{1,0:T(8,128)} %param.3) | copy-start | bytes 1548292
  402.0 0.9 copy-start.4
  402.0 57.9 %copy-start.5 = (bf16[112,1152]{1,0:T(8,128)(2,1)S(1)}, bf16[112,1152]{1,0:T(8,128)(2,1)}, u32[]{:S(2)}) copy-start(bf16[112,1152]{1,0:T(8,128)(2,1)} %param.4) | copy-start | bytes 774148
  463.4 376.0 %all-gather.3.cloned.1.call-start = ((), (), s32[]{:S(2)}) async-start(), calls=%async_computation.2 | async-start | bytes 3194880 | tf_op jit(solution)/shard_map/all_gather | solution.py:39
  843.0 4.9 copy-start.1
Sparse Core Ops, SparseCore 0:
  12.7 131.4 all-reduce.7
  148.3 168.0 all-reduce.9
  463.5 174.7 all-reduce.11
  756.0 83.4 all-gather.2
where the time goes:
time: 865 us; the launch traced here: 861 us
  waiting for transfers between devices  557 us (64%)
  other arithmetic  118 us (14%)
  blocking collectives  115 us (13%)
  matrix products  28.4 us (3%)
  local copies, waits for them, and re-layouts  24.5 us (3%)
  between operations  17.2 us (2%)
    unnamed x5, waiting for transfers between devices  173 us
    psum x1, waiting for transfers between devices, per_device(): inner = lax.psum(mult(projected.T, projected), 'fsdp')  168 us
    psum x1, waiting for transfers between devices, per_device(): projected = lax.psum(partial_rows, 'tp')  132 us
    psum x1, blocking collectives, per_device(): lax.psum(jnp.sum(right_rows * right_rows, axis=0), ('fsdp', 'tp')) + epsilon  115 us
    all_gather x1, waiting for transfers between devices, per_device(): gathered = lax.all_gather(factor_rows, 'fsdp', axis=0, tiled=True)  83.6 us
    another operation x14, other arithmetic, per_device(): triangle = jnp.linalg.cholesky(inner)  72.8 us
    another operation x7, other arithmetic, make_orthonormal(): jax.scipy.linalg.solve_triangular(triangle, rows_block.T, lower=True)  41.9 us
    dot_general x5, matrix products, mult(): return jnp.dot(left, right, precision=lax.Precision.HIGHEST)  18.2 us
  transfers between devices with their start and end apart: 4, of which 4 were waited for; matrix products, arithmetic and copies ran while one was open for 0% of the time, Pallas kernels for 0%

commit v1 on v0

v1 whole, which is shorter than its diff:
```python
import math

import jax
import jax.numpy as jnp
from jax import lax
from jax.experimental import pallas as pl
from jax.experimental.pallas import tpu as pltpu
from jax.sharding import PartitionSpec as P

MESH = pl.DeviceIdType.MESH
F32 = jnp.float32
BF16 = jnp.bfloat16
M_ROWS = 7168
N_COLS = 18432
RANK = 448
ROWS = 112
COLS = 1152
HALF = 56
PAD = 512
momentum_decay = 0.95
epsilon = 1e-08

STREAMS = (
    ("x", 0, 384, 4, 3),
    ("x", 384, 256, 3, 4),
    ("z", 640, 256, 4, 3),
    ("z", 896, 256, 3, 4),
)


def split(a):
    high = a.astype(BF16)
    return high, (a - high.astype(F32)).astype(BF16)


def dot3(a, b, dims):
    ah, al = split(a)
    bh, bl = split(b)

    def one(u, v):
        return lax.dot_general(u, v, (dims, ((), ())), preferred_element_type=F32)

    return one(ah, bh) + (one(ah, bl) + one(al, bh))


def dot_high(a, b, dims):
    return lax.dot_general(
        a, b, (dims, ((), ())), preferred_element_type=F32, precision=lax.Precision.HIGHEST
    )


class Place:
    def __init__(self):
        f, t = lax.axis_index("fsdp"), lax.axis_index("tp")
        self.at = dict(z=f // 8, x=f % 8, y=t // 2, core=t % 2)

    def device(self, **delta):
        at = {k: (v + delta.get(k, 0)) % (2 if k == "core" else 8) for k, v in self.at.items()}
        return (at["z"] * 8 + at["x"], at["y"] * 2 + at["core"])

    def step(self, axis, d):
        return (self.at[axis] + d) % 8


class Copies:
    def __init__(self, send_sem, recv_sem):
        self.send_sem, self.recv_sem, self.used, self.all = send_sem, recv_sem, 0, []

    def start(self, src, dst, device):
        n = self.used
        self.used += 1
        copy = pltpu.make_async_remote_copy(
            src_ref=src,
            dst_ref=dst,
            send_sem=self.send_sem.at[n],
            recv_sem=self.recv_sem.at[n],
            device_id=device,
            device_id_type=MESH,
        )
        copy.start()
        self.all.append(copy)
        return copy

    def finish(self):
        for copy in self.all:
            copy.wait_send()


def rows_at(start, size):
    return pl.ds(pl.multiple_of(start, 8), size)


SEMS = 200


def sums_kernel(
    mom_ref, grad_ref, fac_ref, p_ref, inner_ref, gt_ref,
    pp, pcore, ph, py, pfull, ip, ix, irx, irz, ifull, gp, gright, gleft, gs, gd, ga,
    send_sem, recv_sem,
):
    here = Place()
    z, x, y, core = (here.at[k] for k in ("z", "x", "y", "core"))
    t = y * 2 + core
    copies = Copies(send_sem, recv_sem)
    barrier = pltpu.get_barrier_semaphore()
    peers = [here.device(core=1)]
    for axis in ("x", "z", "y"):
        peers += [here.device(**{axis: d}) for d in range(1, 8)]
    for peer in peers:
        pl.semaphore_signal(barrier, inc=1, device_id=peer, device_id_type=MESH)

    buffer = mom_ref[...] + grad_ref[...].astype(F32)
    partial = dot3(buffer, fac_ref[...], ((1,), (0,)))
    pp[0, :HALF] = partial[:HALF]
    pp[1, :HALF] = partial[HALF:]
    pp[:, HALF:] = jnp.zeros((2, 8, RANK), F32)
    pl.semaphore_wait(barrier, len(peers))

    sibling = here.device(core=1)
    c = copies.start(pp.at[1 - core], pcore, sibling)
    c.wait_recv()
    ph[...] = pp[core] + pcore[...]
    cs = []
    for d in range(1, 8):
        cs.append(copies.start(ph.at[rows_at(8 * here.step("y", d), 8)], py.at[d - 1], here.device(y=d)))
    for c in cs:
        c.wait_recv()
    total = ph[rows_at(8 * y, 8), :]
    for d in range(7):
        total = total + py[d]
    pfull[core, rows_at(8 * y, 8), :] = total
    cs = []
    tile = pfull.at[core, rows_at(8 * y, 8)]
    for d in range(1, 8):
        cs.append(copies.start(tile, tile, here.device(y=d)))
    for c in cs:
        c.wait_recv()
    copies.start(pfull.at[core], pfull.at[core], sibling).wait_recv()
    projected = jnp.concatenate([pfull[0, :HALF], pfull[1, :HALF]], axis=0)
    p_ref[...] = projected

    ip[...] = jnp.zeros((PAD, PAD), F32)
    ip[:RANK, :RANK] = dot_high(projected, projected, ((0,), (0,)))

    def chunk(k):
        return (
            rows_at(32 * t + 8 * (k // 2), 8),
            pl.ds(pl.multiple_of(256 * (k % 2), 256), 256),
        )

    inner_x = []
    for d in range(1, 8):
        r, l = chunk(here.step("x", d))
        inner_x.append(copies.start(ip.at[r, l], irx.at[d - 1], here.device(x=d)))

    gp[...] = dot3(projected, buffer, ((0,), (0,)))
    arrived = {}

    def ring_send(s):
        for n, (axis, lane, lanes, rights, lefts) in enumerate(STREAMS):
            ls = pl.ds(lane, lanes)
            for sign, count, store in ((1, rights, gright), (-1, lefts, gleft)):
                if s > count:
                    continue
                own = rows_at(HALF * here.step(axis, sign * (count + 1 - s)), HALF)
                if s == 1:
                    src = gp.at[own, ls]
                else:
                    arrived[n, sign].wait_recv()
                    store[s - 2, :, ls] += gp[own, ls]
                    src = store.at[s - 2, :, ls]
                arrived[n, sign] = copies.start(src, store.at[s - 1, :, ls], here.device(**{axis: sign}))

    ring_send(1)
    for c in inner_x:
        c.wait_recv()
    r, l = chunk(x)
    total = ip[r, l]
    for d in range(7):
        total = total + irx[d]
    ix[...] = total
    inner_z = []
    for d in range(1, 8):
        inner_z.append(copies.start(ix, irz.at[d - 1], here.device(z=d)))
    ring_send(2)
    for c in inner_z:
        c.wait_recv()
    total = jnp.zeros((8, 256), F32)
    irz[7] = ix[...]
    for k in range(8):
        total = total + irz[(z - k + 7) % 8]
    mine = (rows_at(8 * (x // 2), 8), pl.ds(pl.multiple_of(256 * (x % 2), 256), 256))
    ifull[y, core, mine[0], mine[1]] = total
    inner_y = []
    part = ifull.at[y, core, mine[0], mine[1]]
    for d in range(1, 8):
        inner_y.append(copies.start(part, part, here.device(y=d)))
    ring_send(3)
    for c in inner_y:
        c.wait_recv()
    inner_x = []
    part = ifull.at[:, core, mine[0], mine[1]]
    for d in range(1, 8):
        inner_x.append(copies.start(part, part, here.device(x=d)))
    ring_send(4)

    final = []
    for n, (axis, lane, lanes, rights, lefts) in enumerate(STREAMS):
        ls = pl.ds(lane, lanes)
        arrived[n, 1].wait_recv()
        arrived[n, -1].wait_recv()
        own = rows_at(HALF * here.at[axis], HALF)
        gs[:HALF, ls] = gp[own, ls] + gright[rights - 1, :, ls] + gleft[lefts - 1, :, ls]
    gs[HALF:] = jnp.zeros((8, COLS), F32)
    for axis, ls in (("z", pl.ds(0, 640)), ("x", pl.ds(640, 512))):
        for d in range(1, 8):
            src = gs.at[rows_at(8 * here.step(axis, d), 8), ls]
            final.append(copies.start(src, gd.at[d - 1, :, ls], here.device(**{axis: d})))
    for c in inner_x:
        c.wait_recv()
    inner_core = copies.start(ifull.at[:, core], ifull.at[:, core], sibling)
    for c in final:
        c.wait_recv()
    back = []
    for ring, axis, ls in (("x", "z", pl.ds(0, 640)), ("z", "x", pl.ds(640, 512))):
        r = rows_at(8 * here.at[axis], 8)
        total = gs[r, ls]
        for d in range(7):
            total = total + gd[d, :, ls]
        ga[here.at[ring], r, ls] = total
        part = ga.at[here.at[ring], r, ls]
        for d in range(1, 8):
            back.append(copies.start(part, part, here.device(**{axis: d})))
    for c in back:
        c.wait_recv()
    for s in range(1, 5):
        for n, (axis, lane, lanes, rights, lefts) in enumerate(STREAMS):
            for sign, count in ((1, rights), (-1, lefts)):
                if s > 1 and s - 1 <= count:
                    arrived[n, sign].wait_recv()
                if s > count:
                    continue
                part = ga.at[here.step(axis, -sign * (s - 1)), pl.ds(0, HALF), pl.ds(lane, lanes)]
                arrived[n, sign] = copies.start(part, part, here.device(**{axis: sign}))
    for n, (axis, lane, lanes, rights, lefts) in enumerate(STREAMS):
        for sign, count in ((1, rights), (-1, lefts)):
            if count == 4:
                arrived[n, sign].wait_recv()
    inner_core.wait_recv()
    inner_ref[...] = ifull[...].reshape(PAD, PAD)[:RANK]
    for k in range(8):
        gt_ref[HALF * k : HALF * (k + 1), :] = ga[k, :HALF]
    copies.finish()


def factor_block(block):
    row = lax.broadcasted_iota(jnp.int32, (64, 64), 0)
    col = lax.broadcasted_iota(jnp.int32, (64, 64), 1)
    eye = jnp.where(row == col, 1.0, 0.0).astype(F32)
    both = jnp.concatenate([block, eye], axis=1)
    tiles = [both[8 * q : 8 * q + 8] for q in range(8)]
    sub = lax.broadcasted_iota(jnp.int32, (8, 128), 0)

    def lane(v, k):
        return jnp.broadcast_to(v[:, k : k + 1], (8, 128))

    def sublane(v, k):
        return jnp.broadcast_to(v[k : k + 1, :], (8, 128))

    for p in range(8):
        cols = {(q, k): lane(tiles[q], 8 * p + k) for q in range(p, 8) for k in range(8)}
        for k in range(8):
            pivot = sublane(cols[p, k], k)
            scale = lax.rsqrt(pivot)
            inverse = scale * scale
            line = sublane(tiles[p], k)
            lead = [sublane(cols[p, j], k) for j in range(k + 1, 8)]
            for q in range(p, 8):
                m = cols[q, k] * inverse
                if q == p:
                    m = jnp.where(sub > k, m, 0.0)
                tiles[q] = tiles[q] - m * line
                for j in range(k + 1, 8):
                    cols[q, j] = cols[q, j] - m * lead[j - k - 1]
            tiles[p] = jnp.where(sub == k, tiles[p] * scale, tiles[p])
    return jnp.concatenate(tiles, axis=0)


def factor_kernel(inner_ref, gt_ref, p_ref, q_ref, right_ref, sq_ref, work, tri):
    work[...] = inner_ref[:, :RANK]
    lanes = lax.broadcasted_iota(jnp.int32, (64, RANK), 1)
    for j in range(7):
        lo, hi = 64 * j, 64 * (j + 1)
        both = factor_block(work[lo:hi, lo:hi])
        inverse = both[:, 64:]
        rows = dot_high(inverse, work[lo:hi, :], ((1,), (0,)))
        parts = [inverse]
        if j > 0:
            parts.insert(0, rows[:, :lo])
        if j < 6:
            parts.append(rows[:, hi:])
        rows = jnp.concatenate(parts, axis=1)
        tri[lo:hi, :] = jnp.where(lanes < hi, rows, 0.0)
        if j < 6:
            down = dot_high(rows[:, hi:], rows, ((0,), (0,)))
            below = work[hi:, :]
            keep = lax.broadcasted_iota(jnp.int32, below.shape, 1)
            below = jnp.where((keep >= lo) & (keep < hi), 0.0, below)
            work[hi:, :] = below - down
    inverse = tri[...]
    q_ref[...] = dot3(p_ref[...], inverse, ((1,), (1,)))
    right = dot3(gt_ref[...], inverse, ((0,), (1,)))
    right_ref[...] = right
    sq_ref[...] = jnp.broadcast_to(jnp.sum(right * right, axis=0, keepdims=True), (8, RANK))


def norms_kernel(sq_ref, out_ref, mine, pair, ys, send_sem, recv_sem):
    here = Place()
    copies = Copies(send_sem, recv_sem)
    barrier = pltpu.get_barrier_semaphore()
    peers = [here.device(core=1)] + [here.device(y=d) for d in range(1, 8)]
    for peer in peers:
        pl.semaphore_signal(barrier, inc=1, device_id=peer, device_id_type=MESH)
    mine[...] = sq_ref[...]
    pl.semaphore_wait(barrier, len(peers))
    copies.start(mine, pair, here.device(core=1)).wait_recv()
    ys[7] = mine[...] + pair[...]
    cs = [copies.start(ys.at[7], ys.at[d - 1], here.device(y=d)) for d in range(1, 8)]
    for c in cs:
        c.wait_recv()
    total = jnp.zeros((8, RANK), F32)
    for k in range(8):
        total = total + ys[(here.at["y"] - k + 7) % 8]
    out_ref[...] = total
    copies.finish()


def outputs_kernel(mom_ref, grad_ref, q_ref, right_ref, sq_ref, nm_ref, up_ref, nf_ref):
    inverse = lax.rsqrt(sq_ref[0:1, :] + epsilon)
    right = right_ref[...]
    nf_ref[...] = right * inverse
    rh, rl = split(right)
    q = q_ref[...]
    scale_factor = math.sqrt(M_ROWS * N_COLS / RANK)
    qh, ql = split(q * (scale_factor * inverse))

    def one(u, v):
        return lax.dot_general(u, v, (((1,), (1,)), ((), ())), preferred_element_type=F32)

    up_ref[...] = one(qh, rh) + (one(qh, rl) + one(ql, rh))
    buffer = mom_ref[...] + grad_ref[...].astype(F32)
    nm_ref[...] = buffer - one((q * (1.0 - momentum_decay)).astype(BF16), rh)


def shape(*dims):
    return jax.ShapeDtypeStruct(dims, F32)


VM = pl.BlockSpec(memory_space=pltpu.VMEM)
LIMIT = 48 * 1024 * 1024


def per_device(momentum, gradient, factor):
    scratch = [
        (2, 64, RANK), (64, RANK), (64, RANK), (7, 8, RANK), (2, 64, RANK),
        (PAD, PAD), (8, 256), (7, 8, 256), (8, 8, 256), (8, 2, 32, PAD),
        (RANK, COLS), (4, HALF, COLS), (4, HALF, COLS), (64, COLS), (7, 8, COLS), (8, 64, COLS),
    ]
    projected, inner, gt = pl.pallas_call(
        sums_kernel,
        out_shape=(shape(ROWS, RANK), shape(RANK, PAD), shape(RANK, COLS)),
        in_specs=[VM] * 3,
        out_specs=(VM,) * 3,
        scratch_shapes=[pltpu.VMEM(s, F32) for s in scratch]
        + [pltpu.SemaphoreType.DMA((SEMS,)), pltpu.SemaphoreType.DMA((SEMS,))],
        compiler_params=pltpu.CompilerParams(
            collective_id=0, has_side_effects=True, vmem_limit_bytes=LIMIT
        ),
        name="sums",
    )(momentum, gradient, factor)
    q, right, squares = pl.pallas_call(
        factor_kernel,
        out_shape=(shape(ROWS, RANK), shape(COLS, RANK), shape(8, RANK)),
        in_specs=[VM] * 3,
        out_specs=(VM,) * 3,
        scratch_shapes=[pltpu.VMEM((RANK, RANK), F32), pltpu.VMEM((RANK, RANK), F32)],
        compiler_params=pltpu.CompilerParams(vmem_limit_bytes=LIMIT),
        name="triangle",
    )(inner, gt, projected)
    squares = pl.pallas_call(
        norms_kernel,
        out_shape=shape(8, RANK),
        in_specs=[VM],
        out_specs=VM,
        scratch_shapes=[pltpu.VMEM((8, RANK), F32), pltpu.VMEM((8, RANK), F32), pltpu.VMEM((8, 8, RANK), F32)]
        + [pltpu.SemaphoreType.DMA((8,)), pltpu.SemaphoreType.DMA((8,))],
        compiler_params=pltpu.CompilerParams(
            collective_id=1, has_side_effects=True, vmem_limit_bytes=LIMIT
        ),
        name="norms",
    )(squares)
    return pl.pallas_call(
        outputs_kernel,
        out_shape=(shape(ROWS, COLS), shape(ROWS, COLS), shape(COLS, RANK)),
        in_specs=[VM] * 5,
        out_specs=(VM,) * 3,
        compiler_params=pltpu.CompilerParams(vmem_limit_bytes=LIMIT),
        name="outputs",
    )(momentum, gradient, q, right, squares)


def solution(mesh):
    in_specs = (P("fsdp", "tp"), P("fsdp", "tp"), P("tp", None))
    out_specs = (P("fsdp", "tp"), P("fsdp", "tp"), P("tp", None))
    return jax.shard_map(
        per_device, mesh=mesh, in_specs=in_specs, out_specs=out_specs, check_vma=False
    )
```

time: 865 us -> 143 us (0.17)
  waiting for transfers between devices: 557 us -> 0 us
  Pallas kernels: 0 us -> 137 us
  other arithmetic: 118 us -> 0 us
  blocking collectives: 115 us -> 0 us
  matrix products: 28.4 us -> 0 us
  local copies, waits for them, and re-layouts: 24.5 us -> 5.14 us
  between operations: 17.2 us -> 0.67 us
    psum x2 -> x0, waiting for transfers between devices: 300 us -> none  [the longest x1 168 us: per_device(): inner = lax.psum(mult(projected.T, projected), 'fsdp')]
    unnamed x5 -> x0, waiting for transfers between devices: 173 us -> none
    pallas_call x0 -> x4, Pallas kernels: none -> 137 us  [the longest x1 98.6 us: per_device(): pl.pallas_call(sums_kernel, out_shape=(shape(ROWS, RANK), shape(RANK, PAD...]
    psum x1 -> x0, blocking collectives: 115 us -> none  [per_device(): lax.psum(jnp.sum(right_rows * right_rows, axis=0), ('fsdp', 'tp')) + epsilon]
    another operation x21 -> x0, other arithmetic: 115 us -> none  [the longest x14 72.8 us: per_device(): triangle = jnp.linalg.cholesky(inner)]
    all_gather x1 -> x0, waiting for transfers between devices: 83.6 us -> none  [per_device(): gathered = lax.all_gather(factor_rows, 'fsdp', axis=0, tiled=True)]
    dot_general x5 -> x0, matrix products: 18.2 us -> none  [mult(): return jnp.dot(left, right, precision=lax.Precision.HIGHEST)]
    another operation x15 -> x0, local copies, waits for them, and re-layouts: 10.8 us -> none
  transfers between devices with their start and end apart: 4 -> 0, of which waited for: 4 -> 0; matrix products, arithmetic and copies ran while one was open for 0% -> 0% of each run, Pallas kernels for 0% -> 0%
where the time goes in v1:
time: 143 us
  Pallas kernels  137 us (96%)
  local copies, waits for them, and re-layouts  5.14 us (4%)
    pallas_call x1, Pallas kernels, per_device(): pl.pallas_call(sums_kernel, out_shape=(shape(ROWS, RANK), shape(RANK, PAD...  98.6 us
    pallas_call x1, Pallas kernels, per_device(): pl.pallas_call(factor_kernel, out_shape=(shape(ROWS, RANK), shape(COLS, R...  21 us
    pallas_call x1, Pallas kernels, per_device(): pl.pallas_call(norms_kernel, out_shape=shape(8, RANK), in_specs=[VM], out...  15 us
    unnamed x5, local copies, waits for them, and re-layouts  3.23 us

profile of v1, /device:TPU:1, one launch (start us, length us, event | category | flops | bytes accessed | tf_op | source)
XLA Modules:
  0.0 142.8 jit_solution(6992695543418400785)
XLA Ops:
  0.6 0.0 copy-start.1
  0.6 0.0 copy-start
  0.7 3.2 %copy.6.fac_ref = f32[1152,448]{1,0:T(8,128)} copy(f32[1152,448]{0,1:T(8,128)} %param.5) | data formatting | bytes 4128768 | tf_op args[2]
  3.9 0.0 copy-done.1
  3.9 0.0 copy-done
  3.9 98.6 %sums.1 = (f32[112,448]{1,0:T(8,128)S(1)}, f32[448,512]{1,0:T(8,128)S(1)}, f32[448,1152]{1,0:T(8,128)S(1)}) custom-call(f32[112,1152]{1,0:T(8,128)S(1)} %copy-done, bf16[112,1152]{1,0:T(8,128)(2,1)S(1)} %copy-done.1, f32[1152,448]{1,0:T(8,128)} %copy.6.fac_ref), custom_call_target="tpu_custom_call" | custom-call | tf_op jit(solution)/shard_map/sums/pallas_call | solution.py:369
  102.4 21.0 %triangle.1 = (f32[112,448]{1,0:T(8,128)S(1)}, f32[1152,448]{1,0:T(8,128)S(1)}, f32[8,448]{1,0:T(8,128)S(1)}) custom-call(f32[448,512]{1,0:T(8,128)S(1)} %get-tuple-element.9.inner_ref, f32[448,1152]{1,0:T(8,128)S(1)} %get-tuple-element.10.gt_ref, f32[112,448]{1,0:T(8,128)S(1)} %get-tuple-element.11.p_ref), custom_call_target="tpu_custom_call" | custom-call | tf_op jit(solution)/shard_map/triangle/pallas_call | solution.py:381
  123.4 15.0 %norms.1.sq_ref = f32[8,448]{1,0:T(8,128)S(1)} custom-call(f32[8,448]{1,0:T(8,128)S(1)} %get-tuple-element.14.sq_ref), custom_call_target="tpu_custom_call" | custom-call | tf_op jit(solution)/shard_map/norms/pallas_call | solution.py:390
  138.4 2.5 %outputs.1 = (f32[112,1152]{1,0:T(8,128)}, f32[112,1152]{1,0:T(8,128)}, f32[1152,448]{1,0:T(8,128)S(1)}) custom-call(f32[112,1152]{1,0:T(8,128)S(1)} %copy-done, bf16[112,1152]{1,0:T(8,128)(2,1)S(1)} %copy-done.1, f32[112,448]{1,0:T(8,128)S(1)} %get-tuple-element.12.q_ref, f32[1152,448]{1,0:T(8,128)S(1)} %get-tuple-element.13.right_ref, ...), custom_call_target="tpu_custom_call" | custom-call | tf_op jit(solution)/shard_map/outputs/pallas_call | solution.py:402
  140.9 1.9 %copy.7 = f32[1152,448]{0,1:T(8,128)} copy(f32[1152,448]{1,0:T(8,128)S(1)} %get-tuple-element.17) | data formatting | bytes 4128768 | tf_op jit(solution)/shard_map/outputs/pallas_call | solution.py:402
Async XLA Ops:
  0.6 3.2 %copy-start.1 = (bf16[112,1152]{1,0:T(8,128)(2,1)S(1)}, bf16[112,1152]{1,0:T(8,128)(2,1)}, u32[]{:S(2)}) copy-start(bf16[112,1152]{1,0:T(8,128)(2,1)} %grad_ref.3) | copy-start | bytes 774148
  0.6 3.2 %copy-start = (f32[112,1152]{1,0:T(8,128)S(1)}, f32[112,1152]{1,0:T(8,128)}, u32[]{:S(2)}) copy-start(f32[112,1152]{1,0:T(8,128)} %mom_ref.3) | copy-start | bytes 1548292

commit v2 on v0

v2 whole, which is shorter than its diff:
```python
import math

import jax
import jax.numpy as jnp
from jax import lax
from jax.experimental import pallas as pl
from jax.experimental.pallas import tpu as pltpu
from jax.sharding import PartitionSpec as P

MESH = pl.DeviceIdType.MESH
F32 = jnp.float32
BF16 = jnp.bfloat16
M_ROWS = 7168
N_COLS = 18432
RANK = 448
ROWS = 112
COLS = 1152
HALF = 56
PAD = 512
momentum_decay = 0.95
epsilon = 1e-08

GROUPS = (
    (("x", 0, 384, 1), ("z", 640, 256, 1)),
    (("x", 384, 256, -1), ("z", 896, 256, -1)),
)


def split(a):
    high = a.astype(BF16)
    return high, (a - high.astype(F32)).astype(BF16)


def dot3(a, b, dims):
    ah, al = split(a)
    bh, bl = split(b)

    def one(u, v):
        return lax.dot_general(u, v, (dims, ((), ())), preferred_element_type=F32)

    return one(ah, bh) + (one(ah, bl) + one(al, bh))


def dot_high(a, b, dims):
    return lax.dot_general(
        a, b, (dims, ((), ())), preferred_element_type=F32, precision=lax.Precision.HIGHEST
    )


class Place:
    def __init__(self):
        f, t = lax.axis_index("fsdp"), lax.axis_index("tp")
        eight, two = jnp.int32(8), jnp.int32(2)
        self.at = dict(z=lax.div(f, eight), x=lax.rem(f, eight), y=lax.div(t, two), core=lax.rem(t, two))
        self.steps = {(k, d): lax.rem(v + d, eight) for k, v in self.at.items() for d in range(8)}
        z, x, y, core = (self.at[k] for k in ("z", "x", "y", "core"))
        self.devices = {}
        for d in range(1, 8):
            self.devices["z", d] = (self.steps["z", d] * 8 + x, t)
            self.devices["x", d] = (z * 8 + self.steps["x", d], t)
            self.devices["y", d] = (f, self.steps["y", d] * 2 + core)
        self.devices["core", 1] = (f, y * 2 + 1 - core)

    def device(self, **delta):
        ((axis, d),) = delta.items()
        return self.devices[axis, d % 8]

    def shift(self, at, k):
        return lax.rem(at + (15 - k), jnp.int32(8))

    def step(self, axis, d):
        return self.steps[axis, d % 8]


class Copies:
    def __init__(self, send_sem, recv_sem):
        self.send_sem, self.recv_sem, self.used, self.all = send_sem, recv_sem, 0, []

    def start(self, src, dst, device):
        n = self.used
        self.used += 1
        copy = pltpu.make_async_remote_copy(
            src_ref=src,
            dst_ref=dst,
            send_sem=self.send_sem.at[n],
            recv_sem=self.recv_sem.at[n],
            device_id=device,
            device_id_type=MESH,
        )
        copy.start()
        self.all.append(copy)
        return copy

    def finish(self):
        for copy in self.all:
            copy.wait_send()
        self.all = []


def rows_at(start, size):
    return pl.ds(pl.multiple_of(start, 8), size)


SEMS = 200
STOP = 0
ORDER = "iabiabiabab"
TURNS = {14: "a", 22: "b", 36: "a", 44: "b"}


def sums_kernel(
    mom, grad, fac, q_ref, right_ref, sq_ref,
    pp, pcore, ph, py, pfull, ip, ix, irx, irz, ifull, gp, gr, gs, gd, ga,
    upper, tri, mine, pair, ys, slab_send, slab_recv, send_sem, recv_sem,
):
    here = Place()
    z, x, y, core = (here.at[k] for k in ("z", "x", "y", "core"))
    t = y * 2 + core
    copies = Copies(send_sem, recv_sem)
    barrier = pltpu.get_barrier_semaphore()
    sibling = here.device(core=1)
    peers = [sibling]
    for axis in ("y", "x", "z"):
        peers += [here.device(**{axis: d}) for d in range(1, 8)]
    for peer in peers:
        pl.semaphore_signal(barrier, inc=1, device_id=peer, device_id_type=MESH)
    ip[...] = jnp.zeros((PAD, PAD), F32)
    gs[...] = jnp.zeros((64, COLS), F32)
    pp[:, HALF:] = jnp.zeros((2, 8, RANK), F32)

    buffer = mom[...] + grad[...].astype(F32)
    partial = dot3(buffer, fac[...], ((1,), (1,)))
    pp[0, :HALF] = partial[:HALF]
    pp[1, :HALF] = partial[HALF:]
    pl.semaphore_wait(barrier, len(peers))
    if STOP == 1:
        return

    copies.start(pp.at[1 - core], pcore, sibling).wait_recv()
    ph[...] = pp[core] + pcore[...]
    cs = []
    for d in range(1, 8):
        cs.append(copies.start(ph.at[rows_at(8 * here.step("y", d), 8)], py.at[d - 1], here.device(y=d)))
    total = ph[rows_at(8 * y, 8), :]
    for d, c in enumerate(cs):
        c.wait_recv()
        total = total + py[d]
    pfull[core, rows_at(8 * y, 8), :] = total
    cs = []
    tile = pfull.at[core, rows_at(8 * y, 8)]
    for d in range(1, 8):
        cs.append(copies.start(tile, tile, here.device(y=d)))
    for c in cs:
        c.wait_recv()
    copies.start(pfull.at[core], pfull.at[core], sibling).wait_recv()
    if STOP == 2:
        copies.finish()
        return

    projected = jnp.concatenate([pfull[0, :HALF], pfull[1, :HALF], jnp.zeros((16, RANK), F32)], axis=0)
    across = jnp.transpose(projected)
    ip[:RANK, :RANK] = dot_high(across, projected, ((1,), (0,)))

    def chunk(k):
        return (
            rows_at(32 * t + 8 * lax.div(k, jnp.int32(2)), 8),
            pl.ds(pl.multiple_of(256 * lax.rem(k, jnp.int32(2)), 256), 256),
        )

    def inner_sum():
        cs = []
        for d in range(1, 8):
            r, l = chunk(here.step("x", d))
            cs.append(copies.start(ip.at[r, l], irx.at[d - 1], here.device(x=d)))
        yield
        r, l = chunk(x)
        total = ip[r, l]
        for d, c in enumerate(cs):
            c.wait_recv()
            total = total + irx[d]
        ix[...] = total
        cs = [copies.start(ix, irz.at[d - 1], here.device(z=d)) for d in range(1, 8)]
        yield
        for c in cs:
            c.wait_recv()
        total = jnp.zeros((8, 256), F32)
        irz[7] = ix[...]
        for k in range(8):
            total = total + irz[here.shift(z, k)]
        r, l = rows_at(8 * lax.div(x, jnp.int32(2)), 8), pl.ds(pl.multiple_of(256 * lax.rem(x, jnp.int32(2)), 256), 256)
        ifull[y, core, r, l] = total
        part = ifull.at[y, core, r, l]
        cs = [copies.start(part, part, here.device(x=d)) for d in range(1, 8)]
        yield
        for c in cs:
            c.wait_recv()
        @pl.when(y < 7)
        def _():
            for d in range(1, 8):
                slab(y, d).start()

        yield

    def slab(place, d=1):
        part = ifull.at[place, core]
        return pltpu.make_async_remote_copy(
            src_ref=part,
            dst_ref=part,
            send_sem=slab_send.at[d - 1],
            recv_sem=slab_recv.at[place],
            device_id=here.device(y=d),
            device_id_type=MESH,
        )

    swaps = {}

    def fetch(j):
        @pl.when(y != j)
        def _():
            slab(j).wait_recv()

        part = ifull.at[j, core]
        swaps[j] = copies.start(part, part, sibling)

    def block_rows(j):
        swaps[j].wait_recv()
        return ifull[j].reshape(64, PAD)[:, :RANK]

    def outer_sum(group):
        def own(axis, d, ls):
            return gp.at[rows_at(HALF * here.step(axis, d), HALF), ls]

        got = []
        for axis, lane, lanes, way in group:
            ls = pl.ds(lane, lanes)
            got.append({
                (slot, by): copies.start(own(axis, to, ls), gr.at[slot, :, ls], here.device(**{axis: by}))
                for slot, to, by in ((0, 3, 1), (1, -3, -1), (2, 4, 2 * way), (3, 1, 1), (4, -1, -1))
            })
        yield
        for (axis, lane, lanes, way), arrived in zip(group, got):
            ls = pl.ds(lane, lanes)
            for (slot, by), c in arrived.items():
                if slot < 3:
                    c.wait_recv()
            for slot, by in ((0, 2), (1, -2)):
                total = gr[slot, :, ls] + own(axis, by, ls)[...]
                if by == 2 * way:
                    total = total + gr[2, :, ls]
                gr[slot, :, ls] = total
                arrived[slot + 5, by] = copies.start(
                    gr.at[slot, :, ls], gr.at[slot + 5, :, ls], here.device(**{axis: by})
                )
        yield
        cs = {}
        for n, ((axis, lane, lanes, way), arrived) in enumerate(zip(group, got)):
            ls = pl.ds(lane, lanes)
            total = own(axis, 0, ls)[...]
            for (slot, by), c in arrived.items():
                if slot >= 3:
                    c.wait_recv()
                    total = total + gr[slot, :, ls]
            gs[:HALF, ls] = total
            other = "z" if axis == "x" else "x"
            for d in (4, 3, 5, 2, 6, 1, 7):
                src = gs.at[rows_at(8 * here.step(other, d), 8), ls]
                cs[n, d] = copies.start(src, gd.at[d - 1, :, ls], here.device(**{other: d}))
        yield
        back = []
        for n, (axis, lane, lanes, way) in enumerate(group):
            ls = pl.ds(lane, lanes)
            other = "z" if axis == "x" else "x"
            r = rows_at(8 * here.at[other], 8)
            total = gs[r, ls]
            for d in range(1, 8):
                cs[n, d].wait_recv()
                total = total + gd[d - 1, :, ls]
            ga[here.at[axis], r, ls] = total
            part = ga.at[here.at[axis], r, ls]
            back += [copies.start(part, part, here.device(**{other: d})) for d in (4, 3, 5, 2, 6, 1, 7)]
        yield

        def pass_on(axis, place, by, ls):
            part = ga.at[here.step(axis, place), pl.ds(0, HALF), ls]
            return copies.start(part, part, here.device(**{axis: by}))

        for c in back:
            c.wait_recv()
        got = []
        for axis, lane, lanes, way in group:
            got.append([pass_on(axis, 0, by, pl.ds(lane, lanes)) for by in (2, -2, 1, -1)])
        yield
        for (axis, lane, lanes, way), arrived in zip(group, got):
            arrived[0].wait_recv()
            arrived[1].wait_recv()
            for place, by in ((2, -1), (-2, 1), (-2 * way, 2 * way)):
                arrived.append(pass_on(axis, place, by, pl.ds(lane, lanes)))
        yield
        for arrived in got:
            for c in arrived[2:]:
                c.wait_recv()
        yield

    inner_steps, outer_steps = inner_sum(), [outer_sum(group) for group in GROUPS]
    todo = dict(i=inner_steps, a=outer_steps[0], b=outer_steps[1])
    pa, pb = split(across)
    padded = jnp.concatenate([buffer, jnp.zeros((16, COLS), F32)], axis=0)
    bh, bl = split(padded)

    def one(u, v):
        return jnp.dot(u, v, preferred_element_type=F32)

    next(inner_steps)
    for n, group in enumerate(GROUPS):
        for axis, lane, lanes, way in group:
            ls = slice(lane, lane + lanes)
            gp[:, ls] = one(pa, bh[:, ls]) + (one(pa, bl[:, ls]) + one(pb, bh[:, ls]))
        if STOP != 3:
            next(outer_steps[n])
    for name in ORDER:
        if STOP != 3 or name == "i":
            next(todo[name])
    fetch(0)
    for n, _ in enumerate(factor(block_rows, upper, tri) if STOP == 0 else range(56)):
        if n % 8 == 3 and n < 48:
            fetch(n // 8 + 1)
        if n in TURNS and STOP != 3:
            next(todo[TURNS[n]])
    if STOP > 0:
        for j in range(7):
            swaps[j].wait_recv()
        copies.finish()

        @pl.when(y < 7)
        def _():
            for d in range(1, 8):
                slab(y, d).wait_send()

        return
    inverse = tri[...]
    grown = jnp.concatenate([ga[k, :HALF] for k in range(8)], axis=0)
    right = dot3(inverse, grown, ((1,), (0,)))
    total = right[:, :128] * right[:, :128]
    for k in range(1, 9):
        total = total + right[:, 128 * k : 128 * (k + 1)] * right[:, 128 * k : 128 * (k + 1)]
    total = jnp.concatenate([total, jnp.zeros((PAD - RANK, 128), F32)], axis=0)
    total = jnp.sum(jnp.transpose(total), axis=0, keepdims=True)
    mine[...] = jnp.concatenate(
        [total[:, 128 * k : 128 * (k + 1)] for k in range(4)] + [jnp.zeros((4, 128), F32)], axis=0
    )
    c = copies.start(mine, pair, sibling)
    right_ref[...] = right
    c.wait_recv()
    ys[7] = mine[...] + pair[...]
    cs = [copies.start(ys.at[7], ys.at[d - 1], here.device(y=d)) for d in range(1, 8)]
    q_ref[...] = dot3(projected[:ROWS], inverse, ((1,), (1,)))
    copies.finish()

    @pl.when(y < 7)
    def _():
        for d in range(1, 8):
            slab(y, d).wait_send()

    for c in cs:
        c.wait_recv()
    total = jnp.zeros((8, 128), F32)
    for k in range(8):
        total = total + ys[here.shift(y, k)]
    sq_ref[...] = total
    copies.finish()


def factor_block(block):
    row = lax.broadcasted_iota(jnp.int32, (64, 64), 0)
    col = lax.broadcasted_iota(jnp.int32, (64, 64), 1)
    rest = jnp.concatenate([block, jnp.where(row == col, 1.0, 0.0).astype(F32)], axis=1)
    done = []
    for p in range(8):
        n = 64 - 8 * p
        below = lax.broadcasted_iota(jnp.int32, (n, 128), 0)
        cols = jnp.stack([jnp.broadcast_to(rest[:, 8 * p + k : 8 * p + k + 1], (n, 128)) for k in range(8)])
        for k in range(8):
            scale = lax.rsqrt(cols[0, k : k + 1])
            m = jnp.where(below > k, cols[0] * (scale * scale), 0.0)
            line = rest[k : k + 1]
            done.append(line * scale)
            rest = rest - m * line
            if k < 7:
                cols = cols[1:] - m[None] * cols[1:, k : k + 1]
        rest = rest[8:]
        yield None
    yield jnp.concatenate(done, axis=0)


def factor(block_rows, upper, tri):
    lanes = lax.broadcasted_iota(jnp.int32, (64, RANK), 1)
    for j in range(7):
        lo, hi = 64 * j, 64 * (j + 1)
        block = block_rows(j)
        if j > 0:
            before = lax.broadcasted_iota(jnp.int32, (lo, RANK), 1)
            down = jnp.where(before < lo, tri[:lo, :], upper[:lo, :])
            block = jnp.where(lanes < lo, 0.0, block) - dot_high(upper[:lo, lo:hi], down, ((0,), (0,)))
        for both in factor_block(block[:, lo:hi]):
            if both is None:
                yield None
        inverse = both[:, 64:]
        rows = dot_high(inverse, block, ((1,), (0,)))
        upper[lo:hi, :] = rows
        parts = [inverse]
        if j > 0:
            parts.insert(0, rows[:, :lo])
        if j < 6:
            parts.append(jnp.zeros((64, RANK - hi), F32))
        tri[lo:hi, :] = jnp.concatenate(parts, axis=1)


def outputs_kernel(mom_ref, grad_ref, q_ref, right_ref, sq_ref, nm_ref, up_ref, nf_ref):
    inverse = lax.rsqrt(sq_ref[...] + epsilon)
    inverse = jnp.concatenate([inverse[k : k + 1] for k in range(4)], axis=1)
    column = jnp.transpose(jnp.broadcast_to(inverse, (128, PAD)))[:RANK, 0:1]
    right = right_ref[...]
    nf_ref[...] = right * column
    rh, rl = split(right)
    q = q_ref[...]
    scale_factor = math.sqrt(M_ROWS * N_COLS / RANK)
    qh, ql = split(q * (scale_factor * inverse[:, :RANK]))

    def one(u, v):
        return jnp.dot(u, v, preferred_element_type=F32)

    up_ref[...] = one(qh, rh) + (one(qh, rl) + one(ql, rh))
    buffer = mom_ref[...] + grad_ref[...].astype(F32)
    nm_ref[...] = buffer - one((q * (1.0 - momentum_decay)).astype(BF16), rh)


def shape(*dims):
    return jax.ShapeDtypeStruct(dims, F32)


VM = pl.BlockSpec(memory_space=pltpu.VMEM)
LIMIT = 48 * 1024 * 1024


def per_device(momentum, gradient, factor_rows):
    scratch = [
        (2, 64, RANK), (64, RANK), (64, RANK), (7, 8, RANK), (2, 64, RANK),
        (PAD, PAD), (8, 256), (7, 8, 256), (8, 8, 256), (8, 2, 32, PAD),
        (RANK, COLS), (7, HALF, COLS), (64, COLS), (7, 8, COLS), (8, 64, COLS),
        (RANK, RANK), (RANK, RANK), (8, 128), (8, 128), (8, 8, 128),
    ]
    q, right, squares = pl.pallas_call(
        sums_kernel,
        out_shape=(shape(ROWS, RANK), shape(RANK, COLS), shape(8, 128)),
        in_specs=[VM] * 3,
        out_specs=(VM,) * 3,
        scratch_shapes=[pltpu.VMEM(s, F32) for s in scratch]
        + [pltpu.SemaphoreType.DMA((7,)), pltpu.SemaphoreType.DMA((8,)), pltpu.SemaphoreType.DMA((SEMS,)), pltpu.SemaphoreType.DMA((SEMS,))],
        compiler_params=pltpu.CompilerParams(
            collective_id=0, has_side_effects=True, vmem_limit_bytes=LIMIT
        ),
        name="sums",
    )(momentum, gradient, factor_rows.T)
    new_momentum, update, new_factor = pl.pallas_call(
        outputs_kernel,
        out_shape=(shape(ROWS, COLS), shape(ROWS, COLS), shape(RANK, COLS)),
        in_specs=[VM] * 5,
        out_specs=(VM,) * 3,
        compiler_params=pltpu.CompilerParams(vmem_limit_bytes=LIMIT),
        name="outputs",
    )(momentum, gradient, q, right, squares)
    return new_momentum, update, new_factor.T


def solution(mesh):
    in_specs = (P("fsdp", "tp"), P("fsdp", "tp"), P("tp", None))
    out_specs = (P("fsdp", "tp"), P("fsdp", "tp"), P("tp", None))
    return jax.shard_map(
        per_device, mesh=mesh, in_specs=in_specs, out_specs=out_specs, check_vma=False
    )
```

time: 865 us -> 110 us (0.13)
  waiting for transfers between devices: 557 us -> 0 us
  other arithmetic: 118 us -> 0 us
  blocking collectives: 115 us -> 0 us
  Pallas kernels: 0 us -> 105 us
  matrix products: 28.4 us -> 0 us
  local copies, waits for them, and re-layouts: 24.5 us -> 3.56 us
  between operations: 17.2 us -> 0.65 us
    psum x2 -> x0, waiting for transfers between devices: 300 us -> none  [the longest x1 168 us: per_device(): inner = lax.psum(mult(projected.T, projected), 'fsdp')]
    unnamed x5 -> x0, waiting for transfers between devices: 173 us -> none
    psum x1 -> x0, blocking collectives: 115 us -> none  [per_device(): lax.psum(jnp.sum(right_rows * right_rows, axis=0), ('fsdp', 'tp')) + epsilon]
    another operation x21 -> x0, other arithmetic: 115 us -> none  [the longest x14 72.8 us: per_device(): triangle = jnp.linalg.cholesky(inner)]
    pallas_call x0 -> x2, Pallas kernels: none -> 105 us  [the longest x1 103 us: per_device(): pl.pallas_call(sums_kernel, out_shape=(shape(ROWS, RANK), shape(RANK, COL...]
    all_gather x1 -> x0, waiting for transfers between devices: 83.6 us -> none  [per_device(): gathered = lax.all_gather(factor_rows, 'fsdp', axis=0, tiled=True)]
    dot_general x5 -> x0, matrix products: 18.2 us -> none  [mult(): return jnp.dot(left, right, precision=lax.Precision.HIGHEST)]
    another operation x15 -> x0, local copies, waits for them, and re-layouts: 10.8 us -> none
  transfers between devices with their start and end apart: 4 -> 0, of which waited for: 4 -> 0; matrix products, arithmetic and copies ran while one was open for 0% -> 0% of each run, Pallas kernels for 0% -> 0%
where the time goes in v2:
time: 110 us; the launch traced here: 109 us
  Pallas kernels  105 us (95%)
  local copies, waits for them, and re-layouts  3.56 us (3%)
    pallas_call x1, Pallas kernels, per_device(): pl.pallas_call(sums_kernel, out_shape=(shape(ROWS, RANK), shape(RANK, COL...  103 us
    unnamed x6, local copies, waits for them, and re-layouts  3.56 us
    pallas_call x1, Pallas kernels, per_device(): pl.pallas_call(outputs_kernel, out_shape=(shape(ROWS, COLS), shape(ROWS,...  2.55 us

profile of v2, /device:TPU:1, one launch (start us, length us, event | category | flops | bytes accessed | tf_op | source)
XLA Modules:
  0.0 109.4 jit_solution(8811898080960742257)
XLA Ops:
  0.6 0.0 copy-start
  0.6 1.6 %copy-done = f32[1152,448]{0,1:T(8,128)S(1)} copy-done((f32[1152,448]{0,1:T(8,128)S(1)}, f32[1152,448]{0,1:T(8,128)}, u32[]{:S(2)}) %copy-start) | copy-done | bytes 2064408
  2.2 0.0 copy-start.1
  2.2 1.0 copy-done.1
  3.2 0.0 copy-start.2
  3.3 0.9 copy-done.2
  4.2 102.6 %sums.1 = (f32[112,448]{1,0:T(8,128)S(1)}, f32[448,1152]{1,0:T(8,128)S(1)}, f32[8,128]{1,0:T(8,128)S(1)}) custom-call(f32[112,1152]{1,0:T(8,128)S(1)} %copy-done.1, bf16[112,1152]{1,0:T(8,128)(2,1)S(1)} %copy-done.2, f32[448,1152]{1,0:T(8,128)S(1)} %bitcast.2), custom_call_target="tpu_custom_call" | custom-call | tf_op jit(solution)/shard_map/sums/pallas_call | solution.py:451
  106.8 2.5 %outputs.1 = (f32[112,1152]{1,0:T(8,128)}, f32[112,1152]{1,0:T(8,128)}, f32[448,1152]{1,0:T(8,128)}) custom-call(f32[112,1152]{1,0:T(8,128)S(1)} %copy-done.1, bf16[112,1152]{1,0:T(8,128)(2,1)S(1)} %copy-done.2, f32[112,448]{1,0:T(8,128)S(1)} %get-tuple-element.9.q_ref, f32[448,1152]{1,0:T(8,128)S(1)} %get-tuple-element.10.right_ref, ...), custom_call_target="tpu_custom_call" | custom-call | tf_op jit(solution)/shard_map/outputs/pallas_call | solution.py:463
Async XLA Ops:
  0.6 1.6 %copy-start = (f32[1152,448]{0,1:T(8,128)S(1)}, f32[1152,448]{0,1:T(8,128)}, u32[]{:S(2)}) copy-start(f32[1152,448]{0,1:T(8,128)} %param.5) | copy-start | bytes 6193156
  2.2 1.0 copy-start.1
  3.2 0.9 copy-start.2

commit v3 on v2

--- a/solution.py
+++ b/solution.py
@@ -102,9 +102,9 @@
 
 
 SEMS = 200
-STOP = 0
-ORDER = "iabiabiabab"
-TURNS = {14: "a", 22: "b", 36: "a", 44: "b"}
+ORDER = "iabiabiab"
+LATER = "a"
+TURNS = {3: "b", 20: "a", 27: "b", 38: "a", 44: "b"}
 
 
 def sums_kernel(
@@ -132,29 +132,26 @@
     pp[0, :HALF] = partial[:HALF]
     pp[1, :HALF] = partial[HALF:]
     pl.semaphore_wait(barrier, len(peers))
-    if STOP == 1:
-        return
-
-    copies.start(pp.at[1 - core], pcore, sibling).wait_recv()
-    ph[...] = pp[core] + pcore[...]
-    cs = []
-    for d in range(1, 8):
-        cs.append(copies.start(ph.at[rows_at(8 * here.step("y", d), 8)], py.at[d - 1], here.device(y=d)))
-    total = ph[rows_at(8 * y, 8), :]
-    for d, c in enumerate(cs):
-        c.wait_recv()
-        total = total + py[d]
-    pfull[core, rows_at(8 * y, 8), :] = total
-    cs = []
-    tile = pfull.at[core, rows_at(8 * y, 8)]
-    for d in range(1, 8):
-        cs.append(copies.start(tile, tile, here.device(y=d)))
-    for c in cs:
-        c.wait_recv()
-    copies.start(pfull.at[core], pfull.at[core], sibling).wait_recv()
-    if STOP == 2:
-        copies.finish()
-        return
+
+    def project():
+        copies.start(pp.at[1 - core], pcore, sibling).wait_recv()
+        ph[...] = pp[core] + pcore[...]
+        cs = []
+        for d in range(1, 8):
+            cs.append(copies.start(ph.at[rows_at(8 * here.step("y", d), 8)], py.at[d - 1], here.device(y=d)))
+        total = ph[rows_at(8 * y, 8), :]
+        for d, c in enumerate(cs):
+            c.wait_recv()
+            total = total + py[d]
+        pfull[core, rows_at(8 * y, 8), :] = total
+        cs = []
+        tile = pfull.at[core, rows_at(8 * y, 8)]
+        for d in range(1, 8):
+            cs.append(copies.start(tile, tile, here.device(y=d)))
+        for c in cs:
+            c.wait_recv()
+        copies.start(pfull.at[core], pfull.at[core], sibling).wait_recv()
+    project()
 
     projected = jnp.concatenate([pfull[0, :HALF], pfull[1, :HALF], jnp.zeros((16, RANK), F32)], axis=0)
     across = jnp.transpose(projected)
@@ -193,15 +190,11 @@
         yield
         for c in cs:
             c.wait_recv()
-        @pl.when(y < 7)
-        def _():
-            for d in range(1, 8):
-                slab(y, d).start()
-
-        yield
-
-    def slab(place, d=1):
-        part = ifull.at[place, core]
+        each_slab(lambda c: c.start())
+        yield
+
+    def slab(place, group, d=1):
+        part = ifull.at[place, core, :, pl.ds(128 * group, PAD - 128 * group)]
         return pltpu.make_async_remote_copy(
             src_ref=part,
             dst_ref=part,
@@ -211,14 +204,22 @@
             device_id_type=MESH,
         )
 
+    def each_slab(act):
+        for group in range(4):
+
+            @pl.when((y >= 2 * group) & (y < min(2 * group + 2, 7)))
+            def _():
+                for d in range(1, 8):
+                    act(slab(y, group, d))
+
     swaps = {}
 
     def fetch(j):
         @pl.when(y != j)
         def _():
-            slab(j).wait_recv()
-
-        part = ifull.at[j, core]
+            slab(j, j // 2).wait_recv()
+
+        part = ifull.at[j, core, :, pl.ds(128 * (j // 2), PAD - 128 * (j // 2))]
         swaps[j] = copies.start(part, part, sibling)
 
     def block_rows(j):
@@ -301,7 +302,8 @@
         yield
 
     inner_steps, outer_steps = inner_sum(), [outer_sum(group) for group in GROUPS]
-    todo = dict(i=inner_steps, a=outer_steps[0], b=outer_steps[1])
+    todo = dict(zip("ab", outer_steps))
+    todo["i"] = inner_steps
     pa, pb = split(across)
     padded = jnp.concatenate([buffer, jnp.zeros((16, COLS), F32)], axis=0)
     bh, bl = split(padded)
@@ -314,31 +316,26 @@
         for axis, lane, lanes, way in group:
             ls = slice(lane, lane + lanes)
             gp[:, ls] = one(pa, bh[:, ls]) + (one(pa, bl[:, ls]) + one(pb, bh[:, ls]))
-        if STOP != 3:
-            next(outer_steps[n])
+        next(outer_steps[n])
     for name in ORDER:
-        if STOP != 3 or name == "i":
-            next(todo[name])
+        next(todo[name])
     fetch(0)
-    for n, _ in enumerate(factor(block_rows, upper, tri) if STOP == 0 else range(56)):
+    for name in LATER:
+        next(todo[name])
+    ready = 64 * 6
+
+    def grown(size):
+        return jnp.concatenate([ga[k, :HALF] for k in range(8)], axis=0)[:size]
+
+    for n, _ in enumerate(factor(block_rows, upper, tri)):
         if n % 8 == 3 and n < 48:
             fetch(n // 8 + 1)
-        if n in TURNS and STOP != 3:
+        if n in TURNS:
             next(todo[TURNS[n]])
-    if STOP > 0:
-        for j in range(7):
-            swaps[j].wait_recv()
-        copies.finish()
-
-        @pl.when(y < 7)
-        def _():
-            for d in range(1, 8):
-                slab(y, d).wait_send()
-
-        return
-    inverse = tri[...]
-    grown = jnp.concatenate([ga[k, :HALF] for k in range(8)], axis=0)
-    right = dot3(inverse, grown, ((1,), (0,)))
+        if n == 48:
+            right_ref[:ready] = dot3(tri[:ready, :ready], grown(ready), ((1,), (0,)))
+    right_ref[ready:] = dot3(tri[ready:], grown(RANK), ((1,), (0,)))
+    inverse, right = tri[...], right_ref[...]
     total = right[:, :128] * right[:, :128]
     for k in range(1, 9):
         total = total + right[:, 128 * k : 128 * (k + 1)] * right[:, 128 * k : 128 * (k + 1)]
@@ -348,18 +345,13 @@
         [total[:, 128 * k : 128 * (k + 1)] for k in range(4)] + [jnp.zeros((4, 128), F32)], axis=0
     )
     c = copies.start(mine, pair, sibling)
-    right_ref[...] = right
     c.wait_recv()
     ys[7] = mine[...] + pair[...]
     cs = [copies.start(ys.at[7], ys.at[d - 1], here.device(y=d)) for d in range(1, 8)]
     q_ref[...] = dot3(projected[:ROWS], inverse, ((1,), (1,)))
     copies.finish()
 
-    @pl.when(y < 7)
-    def _():
-        for d in range(1, 8):
-            slab(y, d).wait_send()
-
+    each_slab(lambda c: c.wait_send())
     for c in cs:
         c.wait_recv()
     total = jnp.zeros((8, 128), F32)
@@ -372,23 +364,34 @@
 def factor_block(block):
     row = lax.broadcasted_iota(jnp.int32, (64, 64), 0)
     col = lax.broadcasted_iota(jnp.int32, (64, 64), 1)
+    diagonal = jnp.where(row == col, block, 0.0)
+    across = lax.rsqrt(jnp.sum(diagonal, axis=0, keepdims=True))
+    block = block * lax.rsqrt(jnp.sum(diagonal, axis=1, keepdims=True)) * across
     rest = jnp.concatenate([block, jnp.where(row == col, 1.0, 0.0).astype(F32)], axis=1)
     done = []
     for p in range(8):
         n = 64 - 8 * p
         below = lax.broadcasted_iota(jnp.int32, (n, 128), 0)
         cols = jnp.stack([jnp.broadcast_to(rest[:, 8 * p + k : 8 * p + k + 1], (n, 128)) for k in range(8)])
-        for k in range(8):
-            scale = lax.rsqrt(cols[0, k : k + 1])
-            m = jnp.where(below > k, cols[0] * (scale * scale), 0.0)
+        for k in range(0, 8, 2):
+            first, both, second = cols[0, k : k + 1], cols[1, k : k + 1], cols[1, k + 1 : k + 2]
+            root = lax.rsqrt(first)
+            root2 = lax.rsqrt(first * second - both * both) * (first * root)
+            inverse = root * root
+            ratio = both * inverse
+            m = jnp.where(below > k, cols[0] * inverse, 0.0)
+            m2 = jnp.where(below > k + 1, (cols[1] - m * both) * (root2 * root2), 0.0)
             line = rest[k : k + 1]
-            done.append(line * scale)
-            rest = rest - m * line
-            if k < 7:
-                cols = cols[1:] - m[None] * cols[1:, k : k + 1]
+            line2 = rest[k + 1 : k + 2] - ratio * line
+            done += [line * root, line2 * root2]
+            rest = rest - m * line - m2 * line2
+            if k < 6:
+                lead = cols[2:, k : k + 1]
+                lead2 = cols[2:, k + 1 : k + 2] - ratio * lead
+                cols = cols[2:] - m[None] * lead - m2[None] * lead2
         rest = rest[8:]
         yield None
-    yield jnp.concatenate(done, axis=0)
+    yield jnp.concatenate(done, axis=0)[:, 64:] * across
 
 
 def factor(block_rows, upper, tri):
@@ -403,7 +406,7 @@
         for both in factor_block(block[:, lo:hi]):
             if both is None:
                 yield None
-        inverse = both[:, 64:]
+        inverse = both
         rows = dot_high(inverse, block, ((1,), (0,)))
         upper[lo:hi, :] = rows
         parts = [inverse]

time: 110 us -> 108 us (0.982)
    pallas_call x1, Pallas kernels: 103 us -> 101 us  [per_device(): pl.pallas_call(sums_kernel, out_shape=(shape(ROWS, RANK), shape(RANK, COL...]
where the time goes in v3:
time: 108 us
  Pallas kernels  104 us (96%)
  local copies, waits for them, and re-layouts  3.56 us (3%)
    pallas_call x1, Pallas kernels, per_device(): pl.pallas_call(sums_kernel, out_shape=(shape(ROWS, RANK), shape(RANK, COL...  101 us
    unnamed x6, local copies, waits for them, and re-layouts  3.56 us
    pallas_call x1, Pallas kernels, per_device(): pl.pallas_call(outputs_kernel, out_shape=(shape(ROWS, COLS), shape(ROWS,...  2.54 us

profile of v3, /device:TPU:1, one launch (start us, length us, event | category | flops | bytes accessed | tf_op | source)
XLA Modules:
  0.0 107.7 jit_solution(17678317052329690973)
XLA Ops:
  0.6 0.0 copy-start
  0.6 1.6 %copy-done = f32[1152,448]{0,1:T(8,128)S(1)} copy-done((f32[1152,448]{0,1:T(8,128)S(1)}, f32[1152,448]{0,1:T(8,128)}, u32[]{:S(2)}) %copy-start) | copy-done | bytes 2064408
  2.2 0.0 copy-start.1
  2.2 1.0 copy-done.1
  3.2 0.0 copy-start.2
  3.3 0.9 copy-done.2
  4.2 101.0 %sums.1 = (f32[112,448]{1,0:T(8,128)S(1)}, f32[448,1152]{1,0:T(8,128)S(1)}, f32[8,128]{1,0:T(8,128)S(1)}) custom-call(f32[112,1152]{1,0:T(8,128)S(1)} %copy-done.1, bf16[112,1152]{1,0:T(8,128)(2,1)S(1)} %copy-done.2, f32[448,1152]{1,0:T(8,128)S(1)} %bitcast.2), custom_call_target="tpu_custom_call" | custom-call | tf_op jit(solution)/shard_map/sums/pallas_call | solution.py:454
  105.2 2.5 %outputs.1 = (f32[112,1152]{1,0:T(8,128)}, f32[112,1152]{1,0:T(8,128)}, f32[448,1152]{1,0:T(8,128)}) custom-call(f32[112,1152]{1,0:T(8,128)S(1)} %copy-done.1, bf16[112,1152]{1,0:T(8,128)(2,1)S(1)} %copy-done.2, f32[112,448]{1,0:T(8,128)S(1)} %get-tuple-element.9.q_ref, f32[448,1152]{1,0:T(8,128)S(1)} %get-tuple-element.10.right_ref, ...), custom_call_target="tpu_custom_call" | custom-call | tf_op jit(solution)/shard_map/outputs/pallas_call | solution.py:466
Async XLA Ops:
  0.6 1.6 %copy-start = (f32[1152,448]{0,1:T(8,128)S(1)}, f32[1152,448]{0,1:T(8,128)}, u32[]{:S(2)}) copy-start(f32[1152,448]{0,1:T(8,128)} %param.5) | copy-start | bytes 6193156
  2.2 1.0 copy-start.1
  3.2 0.9 copy-start.2
